TPU v7x, 256 devices: a whole 4x4x8 slice. The times are simulated.
256 devices in a mesh: gx: 32 (over z, x_hi, core), gy: 8 (over y, x_lo).
Axes of the slice: x: 4 (x_hi: 2, x_lo: 2; x = x_hi * 2 + x_lo), y: 4, z: 8, core: 2. Of those that a mesh axis runs over, the one named last changes fastest.
Arguments:
- start: float32 [19, 2, 256, 4096], P(None, None, 'gx', 'gy'), may hold values from 0 to 1, as said below
- final_adjoint: float32 [19, 2, 256, 4096], P(None, None, 'gx', 'gy'), may hold values from -6 to 6
- resist: float32 [2, 256, 4096], P(None, 'gx', 'gy'), may hold values from 0.05 to 3
- mask: int32 [2, 256, 4096], P(None, 'gx', 'gy'), may hold values 0 or 1
Outputs:
- adjoint_start: float32 [19, 2, 256, 4096], P(None, None, 'gx', 'gy')
- resist_grad: float32 [2, 256, 4096], P(None, 'gx', 'gy')
Inputs may be any that keep to these rules, and one draw needn't show every extreme that they name: `start`: every population is positive, within a factor 0.5 to 1.5 of its lattice weight.
All inputs are finite; a program needn't handle non-finite values. No bound on the sum of `mask` on one device may be relied on, other than what follows from the above.
Results may differ from a plain program's by a relative error of at most 0.0003.
Values sent between devices are 32-bit elements; how exact they have to be, the bound alone decides.
A program may use at most 64 MiB of HBM per device.

v0:
```python
import functools

import jax
import jax.numpy as jnp
from jax import lax
from jax.experimental import pallas as pl
from jax.experimental.pallas import tpu as pltpu
from jax.sharding import PartitionSpec as P

MESH = pl.DeviceIdType.MESH
F32 = jnp.float32
OMEGA = 1.25
KEEP = 1.0 - OMEGA

LINKS = [
    (0, 0, 0),
    (1, 0, 0), (-1, 0, 0), (0, 1, 0), (0, -1, 0), (0, 0, 1), (0, 0, -1),
    (1, 1, 0), (-1, -1, 0), (1, -1, 0), (-1, 1, 0),
    (1, 0, 1), (-1, 0, -1), (1, 0, -1), (-1, 0, 1),
    (0, 1, 1), (0, -1, -1), (0, 1, -1), (0, -1, 1),
]
Q = 19
UP = [1, 7, 9, 11, 13]
FLAT = [0, 3, 4, 5, 6, 15, 16, 17, 18]
DOWN = [2, 8, 10, 12, 14]
DRAG, SOLID, ITEMS = 14, 15, 21
POST = {q: k for k, q in enumerate(UP + FLAT)} | {q: 16 + k for k, q in enumerate(DOWN)}
ADJ = {q: k for k, q in enumerate(UP + FLAT + DOWN)}

ROWS = 8
COLS = 6
SLOTS = 10
PACK = 4


def mask_lanes(low, high, period):
    lane = lax.broadcasted_iota(jnp.int32, (8, 128), 1) % period
    return (lane >= low) & (lane < high)


def row_at(ref, item, row):
    return ref[item, pl.ds(pl.multiple_of((row + 8) * 8, 8), 8), :]


def set_row(ref, item, row, value):
    ref[item, pl.ds(pl.multiple_of((row + 8) * 8, 8), 8), :] = value


def shift_row(value, dy, dz):
    if dz:
        value = pltpu.roll(value, 4, 0)
    if dy:
        lane = lax.broadcasted_iota(jnp.int32, (8, 128), 1)
        moved = pltpu.roll(value, dy % 128, 1)
        beside = pltpu.roll(moved, dy % 8, 0)
        value = jnp.where(lane == (0 if dy > 0 else 127), beside, moved)
    return value


def shift_strip(value, dx, dy, dz):
    if dx:
        value = pltpu.roll(value, dx % 24, 0)
    turn = (dy + 64 * abs(dz)) % 128
    if turn:
        value = pltpu.roll(value, turn, 1)
    return value


def moments(f, drag):
    total = {}
    diff = {}
    for q in range(1, Q, 2):
        total[q] = f[q] + f[q + 1]
        diff[q] = f[q] - f[q + 1]
    rho = f[0] + ((total[1] + total[3]) + (total[5] + total[7])) + (
        (total[9] + total[11]) + (total[13] + (total[15] + total[17]))
    )
    scale = drag / rho
    ux = ((diff[1] + diff[7]) + (diff[9] + diff[11]) + diff[13]) * scale
    uy = ((diff[3] + diff[7]) + (diff[15] - diff[9]) + diff[17]) * scale
    uz = ((diff[5] + diff[11]) + (diff[15] - diff[13]) - diff[17]) * scale
    return rho, ux, uy, uz


def along(vec, q):
    out = None
    for part, c in zip(vec, LINKS[q]):
        if c:
            if out is None:
                out = part
            else:
                out = out + part if c > 0 else out - part
    return out


def relax(f, rho, u, solid):
    w2 = rho * (OMEGA / 36.0)
    b = [x * (w2 * 3.0) for x in u]
    h = [x * 1.5 for x in u]
    base = w2 - (u[0] * b[0] + u[1] * b[1] + u[2] * b[2]) * 0.5
    blocked = solid > 0.5
    post = {}
    post[0] = jnp.where(blocked, f[0], KEEP * f[0] + 12.0 * base)
    twice = base + base
    for q in range(1, Q, 2):
        cb, ch = along(b, q), along(h, q)
        if q < 7:
            cb = cb + cb
            even = twice + cb * ch
        else:
            even = base + cb * ch
        post[q] = jnp.where(blocked, f[q + 1], KEEP * f[q] + (even + cb))
        post[q + 1] = jnp.where(blocked, f[q], KEEP * f[q + 1] + (even - cb))
    return post


def pull(inc, rho, u, drag, solid):
    ux, uy, uz = u
    blocked = solid > 0.5
    s, d = {}, {}
    for q in range(1, Q, 2):
        s[q] = inc[q] + inc[q + 1]
        d[q] = inc[q] - inc[q + 1]
    sxy, sxz, syz = s[7] + s[9], s[11] + s[13], s[15] + s[17]
    kxx = (s[1] + s[1]) + sxy + sxz
    kyy = (s[3] + s[3]) + sxy + syz
    kzz = (s[5] + s[5]) + sxz + syz
    kxy, kxz, kyz = s[7] - s[9], s[11] - s[13], s[15] - s[17]
    k0 = 12.0 * inc[0] + 2.0 * (s[1] + s[3] + s[5]) + (sxy + sxz + syz)
    kx = (d[1] + d[1]) + (d[7] + d[9]) + (d[11] + d[13])
    ky = (d[3] + d[3]) + (d[7] - d[9]) + (d[15] + d[17])
    kz = (d[5] + d[5]) + (d[11] - d[13]) + (d[15] - d[17])
    wk = OMEGA / 36.0
    vx = kxx * ux + kxy * uy + kxz * uz
    vy = kxy * ux + kyy * uy + kyz * uz
    vz = kxz * ux + kyz * uy + kzz * uz
    gx = 3.0 * (kx - k0 * ux) + 9.0 * vx
    gy = 3.0 * (ky - k0 * uy) + 9.0 * vy
    gz = 3.0 * (kz - k0 * uz) + 9.0 * vz
    uu = ux * ux + uy * uy + uz * uz
    uku = ux * vx + uy * vy + uz * vz
    grho = wk * (k0 + 1.5 * (k0 * uu) - 4.5 * uku)
    ku = kx * ux + ky * uy + kz * uz
    du = 3.0 * (ku - k0 * uu) + 9.0 * uku
    scale = wk * drag
    g = (gx * scale, gy * scale, gz * scale)
    back = jnp.where(blocked, 0.0, (rho * du) * (-scale))
    out = {0: jnp.where(blocked, inc[0], KEEP * inc[0] + grho)}
    for q in range(1, Q, 2):
        cg = along(g, q)
        out[q] = jnp.where(blocked, inc[q + 1], KEEP * inc[q] + (grho + cg))
        out[q + 1] = jnp.where(blocked, inc[q], KEEP * inc[q + 1] + (grho - cg))
    return out, back


def kernel(
    n_gx, n_gy, start_hbm, adj_hbm, resist_hbm, mask_hbm, out_ref, grad_ref,
    start, adj, resist, mask, p0, p1, p2, q0, q1, q2, q3, m0, m1, m2, m3, sums,
    s0, s1, s2, t0, t1, t2, t3, k0, k1, k2, k3, back_strip, packs, got,
    load_sem, send_sem, recv_sem,
):
    gx, gy = lax.axis_index("gx"), lax.axis_index("gy")

    def device(dx, dy):
        return (lax.rem(gx + dx + n_gx, n_gx), lax.rem(gy + dy + n_gy, n_gy))

    around = [(dx, dy) for dx in (-1, 0, 1) for dy in (-1, 0, 1) if dx or dy]
    barrier = pltpu.get_barrier_semaphore()
    for dx, dy in around:
        pl.semaphore_signal(barrier, inc=1, device_id=device(dx, dy), device_id_type=MESH)

    loads = [
        pltpu.make_async_copy(src, dst, load_sem.at[k])
        for k, (src, dst) in enumerate(
            ((start_hbm, start), (resist_hbm, resist), (mask_hbm, mask), (adj_hbm, adj))
        )
    ]
    for copy in loads:
        copy.start()
    for copy in loads[:3]:
        copy.wait()

    def first(k, _):
        here = pl.ds(pl.multiple_of(k * 8, 8), 8)
        there = pl.ds(64 + k, 8, stride=8)
        f = {q: start[q, here, :] for q in range(Q)}
        drag = 1.0 / (1.0 + resist[here, :])
        solid = mask[here, :].astype(F32)
        rho, *u = moments(f, drag)
        post = relax(f, rho, u, solid)
        for q in range(Q):
            p0[POST[q], there, :] = post[q]
        p0[DRAG, there, :] = drag
        p0[SOLID, there, :] = solid
        for item, value in enumerate((rho, *u)):
            m0[item, there, :] = value
        return 0

    lax.fori_loop(0, 8, first, 0, unroll=4)
    loads[3].wait()

    def turn(k, _):
        here = pl.ds(pl.multiple_of(k * 8, 8), 8)
        there = pl.ds(64 + k, 8, stride=8)
        for q in range(Q):
            q0[ADJ[q], there, :] = adj[q, here, :]
        return 0

    lax.fori_loop(0, 8, turn, 0)

    low0, low1, low2 = mask_lanes(0, 32, 128), mask_lanes(64, 96, 128), mask_lanes(32, 64, 128)

    def own_strip(src, item, tile):
        def part(k, by):
            return pltpu.roll(src[item, pl.ds(tile * 64 + k, 8, stride=8), :], by, 1)

        return jnp.where(
            low0, part(0, 6), jnp.where(low1, part(4, 70), jnp.where(low2, part(3, 44), part(7, 108)))
        )

    sides = [[None] * PACK, [None] * PACK]
    for item in range(ITEMS + Q):
        slot, place = item % SLOTS, item // SLOTS
        src, dst, index = (p0, s0, item) if item < ITEMS else (q0, t0, item - ITEMS)
        strip = own_strip(src, index, 1)
        dst[index, 8:16, :] = strip
        chosen = mask_lanes(slot * COLS, slot * COLS + COLS, 64)
        for side, lane in ((0, 6), (1, 38)):
            moved = pltpu.roll(strip, (slot * COLS - lane) % 128, 1)
            old = sides[side][place]
            sides[side][place] = moved if old is None else jnp.where(chosen, moved, old)
    for side in range(2):
        for place in range(PACK):
            packs[side, place] = sides[side][place]

    pl.semaphore_wait(barrier, len(around))

    copies = []

    def send(src, dst, dx, dy):
        k = len(copies)
        copy = pltpu.make_async_remote_copy(
            src_ref=src, dst_ref=dst, send_sem=send_sem.at[k], recv_sem=recv_sem.at[k],
            device_id=device(dx, dy), device_id_type=MESH,
        )
        copy.start()
        copies.append(copy)

    def span(ref, low, high, row, count):
        return ref.at[pl.ds(low, high - low), pl.ds((row + 8) * 8, count * 8), :]

    def both(ref, low, high, row, count, dx):
        send(span(ref, low, high, row, count), span(ref, low, high, row - 8 * dx, count), dx, 0)

    for dx, dy in around:
        if dy:
            send(packs.at[(dy + 1) // 2], got.at[1 - dx, (1 - dy) // 2], dx, dy)
    both(p0, 0, 21, 4, 4, 1)
    both(p0, 0, 21, 0, 4, -1)
    both(p0, 0, 16, 3, 1, 1)
    both(p0, 5, 21, 4, 1, -1)
    both(p0, 0, 5, 2, 1, 1)
    both(p0, 16, 21, 5, 1, -1)
    posts = len(copies)
    both(q0, 0, 19, 6, 2, 1)
    both(q0, 0, 19, 0, 2, -1)
    both(q0, 5, 19, 5, 1, 1)
    both(q0, 0, 14, 2, 1, -1)
    both(q0, 14, 19, 4, 1, 1)
    both(q0, 0, 5, 3, 1, -1)

    def forward(src, dst, mom, row):
        f = {
            q: shift_row(row_at(src, POST[q], row - LINKS[q][0]), LINKS[q][1], LINKS[q][2])
            for q in range(Q)
        }
        rho, *u = moments(f, row_at(p0, DRAG, row))
        for item, value in enumerate((rho, *u)):
            set_row(mom, item, row, value)
        if dst is not None:
            post = relax(f, rho, u, row_at(p0, SOLID, row))
            for q in range(Q):
                set_row(dst, POST[q], row, post[q])

    def backward(src, dst, mom, row):
        inc = {
            q: shift_row(row_at(src, ADJ[q], row + LINKS[q][0]), -LINKS[q][1], LINKS[q][2])
            for q in range(Q)
        }
        rho, *u = [row_at(mom, item, row) for item in range(4)]
        return pull(inc, rho, u, row_at(p0, DRAG, row), row_at(p0, SOLID, row))

    def middle(src, dst, mom, row):
        out, back = backward(src, dst, mom, row)
        for q in range(Q):
            set_row(dst, ADJ[q], row, out[q])
        place = pl.ds(pl.multiple_of((row + 8) * 8, 8), 8)
        sums[place, :] = back if mom is m3 else sums[place, :] + back

    def rows(body, low, high, *refs):
        def one(row, _):
            body(*refs, row)
            return 0

        lax.fori_loop(low, high, one, 0, unroll=4)

    def rim(body, low, high, *refs):
        n = high - low

        def one(k, _):
            body(*refs, jnp.where(k < n, k + low, 7 - low + n - k))
            return 0

        lax.fori_loop(0, 2 * n, one, 0, unroll=4)

    rows(forward, 1, 7, p0, p1, m1)
    rows(forward, 2, 6, p1, p2, m2)
    rows(forward, 3, 5, p2, None, m3)

    for copy in copies[:posts]:
        copy.wait_recv()
    rim(forward, -5, 1, p0, p1, m1)
    rim(forward, -4, 2, p1, p2, m2)
    rim(forward, -3, 3, p2, None, m3)

    left, right = mask_lanes(0, COLS, 64), mask_lanes(44, 44 + COLS, 64)

    def halo_strip(strip, tile, item, slot, place):
        by = slot * COLS
        low = pltpu.roll(got[tile, 0, place], (-by) % 128, 1)
        high = pltpu.roll(got[tile, 1, place], (44 - by) % 128, 1)
        return jnp.where(left, low, jnp.where(right, high, strip))

    def fill_strips(src, dst, first_item, count):
        for item in range(count):
            slot, place = (first_item + item) % SLOTS, (first_item + item) // SLOTS
            for tile in range(3):
                strip = dst[item, 8:16, :] if tile == 1 else own_strip(src, item, tile)
                dst[item, 8 * tile : 8 * tile + 8, :] = halo_strip(strip, tile, item, slot, place)

    fill_strips(p0, s0, 0, ITEMS)

    def strip_forward(src, dst, mom):
        f = {q: shift_strip(src[POST[q]], *LINKS[q]) for q in range(Q)}
        rho, *u = moments(f, s0[DRAG])
        for item, value in enumerate((rho, *u)):
            mom[item] = value
        if dst is not None:
            post = relax(f, rho, u, s0[SOLID])
            for q in range(Q):
                dst[POST[q]] = post[q]

    for item in range(4):
        k0[item, 8:16, :] = own_strip(m0, item, 1)
    strip_forward(s0, s1, k1)
    strip_forward(s1, s2, k2)
    strip_forward(s2, None, k3)

    def strip_backward(src, mom):
        inc = {q: shift_strip(src[ADJ[q]], *[-c for c in LINKS[q]]) for q in range(Q)}
        rho, *u = [mom[item] for item in range(4)]
        return pull(inc, rho, u, s0[DRAG], s0[SOLID])

    def strip_middle(src, dst, mom):
        out, back = strip_backward(src, mom)
        for q in range(Q):
            dst[ADJ[q]] = out[q]
        back_strip[...] = back if mom is k3 else back_strip[...] + back

    rows(middle, 1, 7, q0, q1, m3)
    rows(middle, 2, 6, q1, q2, m2)
    rows(middle, 3, 5, q2, q3, m1)

    for copy in copies[posts:]:
        copy.wait_recv()
    fill_strips(q0, t0, ITEMS, Q)
    strip_middle(t0, t1, k3)
    strip_middle(t1, t2, k2)
    strip_middle(t2, t3, k1)
    strip_out, strip_back = strip_backward(t3, k0)
    for q in range(Q):
        t1[ADJ[q], 8:16, :] = strip_out[q][8:16]
    back_strip[8:16, :] = back_strip[8:16, :] + strip_back[8:16]

    rim(middle, -3, 1, q0, q1, m3)
    rim(middle, -2, 2, q1, q2, m2)
    rim(middle, -1, 3, q2, q3, m1)

    def final(row, _):
        out, back = backward(q3, None, m0, row)
        there = pl.ds(row, 8, stride=8)
        for q in range(Q):
            out_ref[q, there, :] = out[q]
        grad_ref[there, :] = row_at_sum(row) + back
        return 0

    def row_at_sum(row):
        return sums[pl.ds(pl.multiple_of((row + 8) * 8, 8), 8), :]

    lax.fori_loop(0, 8, final, 0, unroll=4)

    edge_low, edge_high = mask_lanes(0, COLS, 128), mask_lanes(128 - COLS, 128, 128)

    def merge(ref, strip):
        for k, lane, chosen in ((0, 6, edge_low), (4, 70, edge_low), (3, 38 - 122, edge_high), (7, 102 - 122, edge_high)):
            here = slice(8 * k, 8 * k + 8)
            ref[here, :] = jnp.where(chosen, pltpu.roll(strip, (-lane) % 128, 1), ref[here, :])

    for q in range(Q):
        merge(out_ref.at[q], t1[ADJ[q], 8:16, :])
    merge(grad_ref, back_strip[8:16, :])

    for copy in copies:
        copy.wait_send()


def to_tiles(a):
    lead = a.shape[:-3]
    n = len(lead)
    a = a.reshape(*lead, 2, 8, 4, 128)
    a = a.transpose(*range(n), n, n + 2, n + 1, n + 3)
    return a.reshape(*lead, 64, 128)


def from_tiles(a):
    lead = a.shape[:-2]
    n = len(lead)
    a = a.reshape(*lead, 2, 4, 8, 128)
    a = a.transpose(*range(n), n, n + 2, n + 1, n + 3)
    return a.reshape(*lead, 2, 8, 512)


def solution(mesh):
    n_gx, n_gy = mesh.shape["gx"], mesh.shape["gy"]

    def local(start, final_adjoint, resist, mask):
        any_space = pl.BlockSpec(memory_space=pl.ANY)
        vmem = pl.BlockSpec(memory_space=pltpu.VMEM)
        buf = lambda *shape: pltpu.VMEM(shape, F32)
        out, grad = pl.pallas_call(
            functools.partial(kernel, n_gx, n_gy),
            out_shape=(
                jax.ShapeDtypeStruct((Q, 64, 128), F32),
                jax.ShapeDtypeStruct((64, 128), F32),
            ),
            in_specs=[any_space] * 4,
            out_specs=[vmem, vmem],
            scratch_shapes=[
                buf(Q, 64, 128), buf(Q, 64, 128), buf(64, 128), pltpu.VMEM((64, 128), jnp.int32),
                buf(ITEMS, 192, 128), buf(ITEMS, 192, 128), buf(ITEMS, 192, 128),
                buf(Q, 192, 128), buf(Q, 192, 128), buf(Q, 192, 128), buf(Q, 192, 128),
                buf(4, 192, 128), buf(4, 192, 128), buf(4, 192, 128), buf(4, 192, 128), buf(192, 128),
                buf(ITEMS, 24, 128), buf(ITEMS, 24, 128), buf(ITEMS, 24, 128),
                buf(Q, 24, 128), buf(Q, 24, 128), buf(Q, 24, 128), buf(Q, 24, 128),
                buf(4, 24, 128), buf(4, 24, 128), buf(4, 24, 128), buf(4, 24, 128), buf(24, 128),
                buf(2, PACK, 8, 128), buf(3, 2, PACK, 8, 128),
                pltpu.SemaphoreType.DMA((4,)),
                pltpu.SemaphoreType.DMA((18,)),
                pltpu.SemaphoreType.DMA((18,)),
            ],
            compiler_params=pltpu.CompilerParams(
                collective_id=0, has_side_effects=True, vmem_limit_bytes=63 * 2**20
            ),
        )(to_tiles(start), to_tiles(final_adjoint), to_tiles(resist), to_tiles(mask))
        return from_tiles(out), from_tiles(grad)

    return jax.shard_map(
        local,
        mesh=mesh,
        in_specs=(
            P(None, None, "gx", "gy"),
            P(None, None, "gx", "gy"),
            P(None, "gx", "gy"),
            P(None, "gx", "gy"),
        ),
        out_specs=(P(None, None, "gx", "gy"), P(None, "gx", "gy")),
        check_vma=False,
    )
```

profile of v0, /device:TPU:1, one launch (start us, length us, event | category | flops | bytes accessed | tf_op | source)
XLA Modules:
  0.0 32.8 jit_solution(5700859589268260311)
XLA Ops:
  0.6 29.6 %shard_map.59 = (f32[19,64,128]{2,1,0:T(8,128)}, f32[64,128]{1,0:T(8,128)}) custom-call(f32[19,64,128]{2,1,0:T(8,128)} %bitcast.30, f32[19,64,128]{2,1,0:T(8,128)} %bitcast.31, f32[64,128]{1,0:T(8,128)} %bitcast.33, s32[64,128]{1,0:T(8,128)} %bitcast.34), custom_call_target="tpu_custom_call" | custom-call | tf_op jit(solution)/shard_map/pallas_call | solution.py:440
  30.2 0.0 copy-start
  30.2 2.0 %copy.8 = f32[19,2,8,512]{3,2,1,0:T(8,128)} copy(f32[19,2,8,512]{3,2,1,0:T(8,128)} %bitcast.32) | data formatting | bytes 1245184
  32.2 0.0 copy-done
  32.2 0.6 %copy.9 = f32[2,8,512]{2,1,0:T(8,128)} copy(f32[2,8,512]{2,1,0:T(8,128)S(1)} %bitcast.35) | data formatting | bytes 65536
Async XLA Ops:
  30.2 2.0 %copy-start = (f32[64,128]{1,0:T(8,128)S(1)}, f32[64,128]{1,0:T(8,128)}, u32[]{:S(2)}) copy-start(f32[64,128]{1,0:T(8,128)} %get-tuple-element.5) | copy-start | bytes 98308
where the time goes:
time: 32.9 us; the launch traced here: 32.8 us
  Pallas kernels  29.6 us (90%)
  local copies, waits for them, and re-layouts  2.58 us (8%)
  between operations  0.65 us (2%)
    pallas_call x1, Pallas kernels, local(): pl.pallas_call(functools.partial(kernel, n_gx, n_gy), out_shape=(jax.Shap...  29.6 us
    unnamed x4, local copies, waits for them, and re-layouts  2.58 us

commit v1 on v0

--- a/solution.py
+++ b/solution.py
@@ -23,9 +23,8 @@
 UP = [1, 7, 9, 11, 13]
 FLAT = [0, 3, 4, 5, 6, 15, 16, 17, 18]
 DOWN = [2, 8, 10, 12, 14]
-DRAG, SOLID, ITEMS = 14, 15, 21
-POST = {q: k for k, q in enumerate(UP + FLAT)} | {q: 16 + k for k, q in enumerate(DOWN)}
-ADJ = {q: k for k, q in enumerate(UP + FLAT + DOWN)}
+DRAG, SOLID, ITEMS = 19, 20, 21
+ADJ = POST = {q: k for k, q in enumerate(UP + FLAT + DOWN)}
 
 ROWS = 8
 COLS = 6
@@ -156,7 +155,7 @@
 def kernel(
     n_gx, n_gy, start_hbm, adj_hbm, resist_hbm, mask_hbm, out_ref, grad_ref,
     start, adj, resist, mask, p0, p1, p2, q0, q1, q2, q3, m0, m1, m2, m3, sums,
-    s0, s1, s2, t0, t1, t2, t3, k0, k1, k2, k3, back_strip, packs, got,
+    s0, s1, s2, t0, t1, t2, t3, k0, k1, k2, k3, back_strip, packs, got, edges, got_edges,
     load_sem, send_sem, recv_sem,
 ):
     gx, gy = lax.axis_index("gx"), lax.axis_index("gy")
@@ -197,6 +196,52 @@
         return 0
 
     lax.fori_loop(0, 8, first, 0, unroll=4)
+    pl.semaphore_wait(barrier, len(around))
+
+    copies = []
+    whole = [(gx != n_gx - 1, gx != 0), (gx == n_gx - 1, gx == 0)]
+
+    def send(src, dst, dx, dy, which=None):
+        k = len(copies)
+        copy = pltpu.make_async_remote_copy(
+            src_ref=src, dst_ref=dst, send_sem=send_sem.at[k], recv_sem=recv_sem.at[k],
+            device_id=device(dx, dy), device_id_type=MESH,
+        )
+        if which is None:
+            copy.start()
+        else:
+            pl.when(whole[which][0])(copy.start)
+        copies.append((copy, which))
+        return copy, which
+
+    def received(*batches):
+        for copy, which in batches:
+            if which is None:
+                copy.wait_recv()
+            else:
+                pl.when(whole[which][1])(copy.wait_recv)
+
+    def sent(*batches):
+        for copy, which in batches:
+            if which is None:
+                copy.wait_send()
+            else:
+                pl.when(whole[which][0])(copy.wait_send)
+
+    def span(ref, low, high, row, count):
+        return ref.at[pl.ds(low, high - low), pl.ds((row + 8) * 8, count * 8), :]
+
+    def both(ref, low, high, row, count, dx, which=None):
+        there = span(ref, low, high, row - 8 * dx, count)
+        return send(span(ref, low, high, row, count), there, dx, 0, which)
+
+    posts = (
+        both(p0, 0, 19, 7, 1, 1), both(p0, 0, 19, 0, 1, -1),
+        both(p0, 19, 21, 5, 3, 1), both(p0, 19, 21, 0, 3, -1),
+        both(p0, 0, 14, 6, 1, 1), both(p0, 5, 19, 1, 1, -1),
+        both(p0, 0, 5, 5, 1, 1), both(p0, 14, 19, 2, 1, -1),
+    )
+
     loads[3].wait()
 
     def turn(k, _):
@@ -233,41 +278,16 @@
         for place in range(PACK):
             packs[side, place] = sides[side][place]
 
-    pl.semaphore_wait(barrier, len(around))
-
-    copies = []
-
-    def send(src, dst, dx, dy):
-        k = len(copies)
-        copy = pltpu.make_async_remote_copy(
-            src_ref=src, dst_ref=dst, send_sem=send_sem.at[k], recv_sem=recv_sem.at[k],
-            device_id=device(dx, dy), device_id_type=MESH,
-        )
-        copy.start()
-        copies.append(copy)
-
-    def span(ref, low, high, row, count):
-        return ref.at[pl.ds(low, high - low), pl.ds((row + 8) * 8, count * 8), :]
-
-    def both(ref, low, high, row, count, dx):
-        send(span(ref, low, high, row, count), span(ref, low, high, row - 8 * dx, count), dx, 0)
-
-    for dx, dy in around:
-        if dy:
-            send(packs.at[(dy + 1) // 2], got.at[1 - dx, (1 - dy) // 2], dx, dy)
-    both(p0, 0, 21, 4, 4, 1)
-    both(p0, 0, 21, 0, 4, -1)
-    both(p0, 0, 16, 3, 1, 1)
-    both(p0, 5, 21, 4, 1, -1)
-    both(p0, 0, 5, 2, 1, 1)
-    both(p0, 16, 21, 5, 1, -1)
-    posts = len(copies)
-    both(q0, 0, 19, 6, 2, 1)
-    both(q0, 0, 19, 0, 2, -1)
-    both(q0, 5, 19, 5, 1, 1)
-    both(q0, 0, 14, 2, 1, -1)
-    both(q0, 14, 19, 4, 1, 1)
-    both(q0, 0, 5, 3, 1, -1)
+    deeper = (
+        both(p0, 14, 19, 6, 1, 1, 1), both(p0, 5, 19, 5, 1, 1, 1), both(p0, 19, 21, 3, 2, 1, 1),
+        both(p0, 0, 19, 4, 1, 1, 1), both(p0, 0, 14, 3, 1, 1, 1), both(p0, 0, 5, 2, 1, 1, 1),
+    )
+
+    strips = [
+        send(packs.at[(dy + 1) // 2], got.at[1 - dx, (1 - dy) // 2], dx, dy)
+        for dx, dy in around
+        if dy
+    ]
 
     def forward(src, dst, mom, row):
         f = {
@@ -302,7 +322,7 @@
             body(*refs, row)
             return 0
 
-        lax.fori_loop(low, high, one, 0, unroll=4)
+        lax.fori_loop(low, high, one, 0, unroll=min(3, high - low))
 
     def rim(body, low, high, *refs):
         n = high - low
@@ -311,18 +331,40 @@
             body(*refs, jnp.where(k < n, k + low, 7 - low + n - k))
             return 0
 
-        lax.fori_loop(0, 2 * n, one, 0, unroll=4)
+        lax.fori_loop(0, 2 * n, one, 0, unroll=min(3, 2 * n))
 
     rows(forward, 1, 7, p0, p1, m1)
     rows(forward, 2, 6, p1, p2, m2)
     rows(forward, 3, 5, p2, None, m3)
 
-    for copy in copies[:posts]:
-        copy.wait_recv()
-    rim(forward, -5, 1, p0, p1, m1)
-    rim(forward, -4, 2, p1, p2, m2)
-    rim(forward, -3, 3, p2, None, m3)
-
+    adjoints = (
+        both(q0, 0, 19, 6, 2, 1), both(q0, 0, 19, 0, 2, -1),
+        both(q0, 5, 19, 5, 1, 1), both(q0, 0, 14, 2, 1, -1),
+        both(q0, 14, 19, 4, 1, 1), both(q0, 0, 5, 3, 1, -1),
+    )
+
+    received(*posts)
+    rim(forward, -2, 1, p0, p1, m1)
+    rim(forward, -1, 2, p1, p2, m2)
+    rim(forward, 0, 3, p2, None, m3)
+
+    rows_of_moments = (
+        both(m3, 0, 4, 5, 3, 1, 0), both(m3, 0, 4, 0, 3, -1),
+        both(m2, 0, 4, 6, 1, 1, 0), both(m2, 0, 4, 1, 1, -1),
+    )
+
+    received(*deeper)
+
+    @pl.when(whole[1][1])
+    def _():
+        def at(lowest, *refs):
+            lax.fori_loop(0, 3, lambda k, _: (forward(*refs, k + lowest), 0)[1], 0, unroll=3)
+
+        at(-5, p0, p1, m1)
+        at(-4, p1, p2, m2)
+        at(-3, p2, None, m3)
+
+    received(*strips)
     left, right = mask_lanes(0, COLS, 64), mask_lanes(44, 44 + COLS, 64)
 
     def halo_strip(strip, tile, item, slot, place):
@@ -355,6 +397,14 @@
     strip_forward(s0, s1, k1)
     strip_forward(s1, s2, k2)
     strip_forward(s2, None, k3)
+    for item in range(4):
+        low, high = slice(3 * item, 3 * item + 3), slice(12 + item, 13 + item)
+        edges[1, low, :], edges[1, high, :] = k3[item, 13:16, :], k2[item, 14:15, :]
+        edges[0, low, :], edges[0, high, :] = k3[item, 8:11, :], k2[item, 9:10, :]
+    strip_moments = [
+        send(edges.at[(dx + 1) // 2], got_edges.at[(1 - dx) // 2], dx, 0, which)
+        for dx, which in ((1, 0), (-1, None))
+    ]
 
     def strip_backward(src, mom):
         inc = {q: shift_strip(src[ADJ[q]], *[-c for c in LINKS[q]]) for q in range(Q)}
@@ -370,21 +420,6 @@
     rows(middle, 1, 7, q0, q1, m3)
     rows(middle, 2, 6, q1, q2, m2)
     rows(middle, 3, 5, q2, q3, m1)
-
-    for copy in copies[posts:]:
-        copy.wait_recv()
-    fill_strips(q0, t0, ITEMS, Q)
-    strip_middle(t0, t1, k3)
-    strip_middle(t1, t2, k2)
-    strip_middle(t2, t3, k1)
-    strip_out, strip_back = strip_backward(t3, k0)
-    for q in range(Q):
-        t1[ADJ[q], 8:16, :] = strip_out[q][8:16]
-    back_strip[8:16, :] = back_strip[8:16, :] + strip_back[8:16]
-
-    rim(middle, -3, 1, q0, q1, m3)
-    rim(middle, -2, 2, q1, q2, m2)
-    rim(middle, -1, 3, q2, q3, m1)
 
     def final(row, _):
         out, back = backward(q3, None, m0, row)
@@ -397,7 +432,37 @@
     def row_at_sum(row):
         return sums[pl.ds(pl.multiple_of((row + 8) * 8, 8), 8), :]
 
-    lax.fori_loop(0, 8, final, 0, unroll=4)
+    def last_rows(low, high):
+        lax.fori_loop(low, high, final, 0, unroll=high - low)
+
+    received(*adjoints)
+    rim(middle, 0, 1, q0, q1, m3)
+    rim(middle, 1, 2, q1, q2, m2)
+    rim(middle, 2, 3, q2, q3, m1)
+    last_rows(3, 5)
+    fill_strips(q0, t0, ITEMS, Q)
+
+    received(*rows_of_moments, *strip_moments)
+
+    def take_edges(side, wide, thin):
+        for item in range(4):
+            low, high = slice(3 * item, 3 * item + 3), slice(12 + item, 13 + item)
+            k3[item, wide, :], k2[item, thin, :] = got_edges[side, low, :], got_edges[side, high, :]
+
+    pl.when(whole[0][1])(lambda: take_edges(0, slice(5, 8), slice(6, 7)))
+    take_edges(1, slice(16, 19), slice(17, 18))
+    rim(middle, -3, 0, q0, q1, m3)
+    strip_middle(t0, t1, k3)
+    rim(middle, -2, 1, q1, q2, m2)
+    strip_middle(t1, t2, k2)
+    rim(middle, -1, 2, q2, q3, m1)
+    strip_middle(t2, t3, k1)
+    strip_out, strip_back = strip_backward(t3, k0)
+    for q in range(Q):
+        t1[ADJ[q], 8:16, :] = strip_out[q][8:16]
+    back_strip[8:16, :] = back_strip[8:16, :] + strip_back[8:16]
+    last_rows(0, 3)
+    last_rows(5, 8)
 
     edge_low, edge_high = mask_lanes(0, COLS, 128), mask_lanes(128 - COLS, 128, 128)
 
@@ -410,8 +475,7 @@
         merge(out_ref.at[q], t1[ADJ[q], 8:16, :])
     merge(grad_ref, back_strip[8:16, :])
 
-    for copy in copies:
-        copy.wait_send()
+    sent(*copies)
 
 
 def to_tiles(a):
@@ -440,8 +504,8 @@
         out, grad = pl.pallas_call(
             functools.partial(kernel, n_gx, n_gy),
             out_shape=(
-                jax.ShapeDtypeStruct((Q, 64, 128), F32),
-                jax.ShapeDtypeStruct((64, 128), F32),
+                pltpu.VMEM((Q, 64, 128), F32),
+                pltpu.VMEM((64, 128), F32),
             ),
             in_specs=[any_space] * 4,
             out_specs=[vmem, vmem],
@@ -453,15 +517,15 @@
                 buf(ITEMS, 24, 128), buf(ITEMS, 24, 128), buf(ITEMS, 24, 128),
                 buf(Q, 24, 128), buf(Q, 24, 128), buf(Q, 24, 128), buf(Q, 24, 128),
                 buf(4, 24, 128), buf(4, 24, 128), buf(4, 24, 128), buf(4, 24, 128), buf(24, 128),
-                buf(2, PACK, 8, 128), buf(3, 2, PACK, 8, 128),
+                buf(2, PACK, 8, 128), buf(3, 2, PACK, 8, 128), buf(2, 16, 128), buf(2, 16, 128),
                 pltpu.SemaphoreType.DMA((4,)),
-                pltpu.SemaphoreType.DMA((18,)),
-                pltpu.SemaphoreType.DMA((18,)),
+                pltpu.SemaphoreType.DMA((32,)),
+                pltpu.SemaphoreType.DMA((32,)),
             ],
             compiler_params=pltpu.CompilerParams(
-                collective_id=0, has_side_effects=True, vmem_limit_bytes=63 * 2**20
+                collective_id=0, has_side_effects=True, vmem_limit_bytes=48 * 2**20
             ),
-        )(to_tiles(start), to_tiles(final_adjoint), to_tiles(resist), to_tiles(mask))
+        )(*[pltpu.with_memory_space_constraint(to_tiles(a), pltpu.HBM) for a in (start, final_adjoint, resist, mask)])
         return from_tiles(out), from_tiles(grad)
 
     return jax.shard_map(

time: 32.9 us -> 28 us (0.85)
  Pallas kernels: 29.6 us -> 25.8 us
  local copies, waits for them, and re-layouts: 2.58 us -> 1.44 us
    pallas_call x1, Pallas kernels: 29.6 us -> 25.8 us  [local(): pl.pallas_call(functools.partial(kernel, n_gx, n_gy), out_shape=(pltpu.VM...]
    unnamed x4 -> x2, local copies, waits for them, and re-layouts: 2.58 us -> 1.44 us
where the time goes in v1:
time: 28 us; the launch traced here: 27.9 us
  Pallas kernels  25.8 us (92%)
  local copies, waits for them, and re-layouts  1.44 us (5%)
  between operations  0.64 us (2%)
    pallas_call x1, Pallas kernels, local(): pl.pallas_call(functools.partial(kernel, n_gx, n_gy), out_shape=(pltpu.VM...  25.8 us
    unnamed x2, local copies, waits for them, and re-layouts  1.44 us

profile of v1, /device:TPU:1, one launch (start us, length us, event | category | flops | bytes accessed | tf_op | source)
XLA Modules:
  0.0 27.9 jit_solution(16177273175399976310)
XLA Ops:
  0.6 25.8 %shard_map.59 = (f32[19,64,128]{2,1,0:T(8,128)S(1)}, f32[64,128]{1,0:T(8,128)S(1)}) custom-call(f32[19,64,128]{2,1,0:T(8,128)} %bitcast.32, f32[19,64,128]{2,1,0:T(8,128)} %bitcast.33, f32[64,128]{1,0:T(8,128)} %bitcast.34, s32[64,128]{1,0:T(8,128)} %bitcast.35), custom_call_target="tpu_custom_call" | custom-call | tf_op jit(solution)/shard_map/pallas_call | solution.py:504
  26.4 0.8 %copy.8 = f32[19,2,8,512]{3,2,1,0:T(8,128)} copy(f32[19,2,8,512]{3,2,1,0:T(8,128)S(1)} %bitcast.30) | data formatting | bytes 1245184
  27.3 0.6 %copy.9 = f32[2,8,512]{2,1,0:T(8,128)} copy(f32[2,8,512]{2,1,0:T(8,128)S(1)} %bitcast.31) | data formatting | bytes 65536

commit v2 on v0

--- a/solution.py
+++ b/solution.py
@@ -23,9 +23,8 @@
 UP = [1, 7, 9, 11, 13]
 FLAT = [0, 3, 4, 5, 6, 15, 16, 17, 18]
 DOWN = [2, 8, 10, 12, 14]
-DRAG, SOLID, ITEMS = 14, 15, 21
-POST = {q: k for k, q in enumerate(UP + FLAT)} | {q: 16 + k for k, q in enumerate(DOWN)}
-ADJ = {q: k for k, q in enumerate(UP + FLAT + DOWN)}
+DRAG, SOLID, ITEMS = 19, 20, 21
+ADJ = POST = {q: k for k, q in enumerate(UP + FLAT + DOWN)}
 
 ROWS = 8
 COLS = 6
@@ -79,7 +78,7 @@
     ux = ((diff[1] + diff[7]) + (diff[9] + diff[11]) + diff[13]) * scale
     uy = ((diff[3] + diff[7]) + (diff[15] - diff[9]) + diff[17]) * scale
     uz = ((diff[5] + diff[11]) + (diff[15] - diff[13]) - diff[17]) * scale
-    return rho, ux, uy, uz
+    return ux, uy, uz, rho
 
 
 def along(vec, q):
@@ -156,7 +155,7 @@
 def kernel(
     n_gx, n_gy, start_hbm, adj_hbm, resist_hbm, mask_hbm, out_ref, grad_ref,
     start, adj, resist, mask, p0, p1, p2, q0, q1, q2, q3, m0, m1, m2, m3, sums,
-    s0, s1, s2, t0, t1, t2, t3, k0, k1, k2, k3, back_strip, packs, got,
+    s0, s1, s2, t0, t1, t2, t3, k0, k1, k2, k3, back_strip, packs, got, edges, got_edges, relay, got_relay,
     load_sem, send_sem, recv_sem,
 ):
     gx, gy = lax.axis_index("gx"), lax.axis_index("gy")
@@ -164,7 +163,7 @@
     def device(dx, dy):
         return (lax.rem(gx + dx + n_gx, n_gx), lax.rem(gy + dy + n_gy, n_gy))
 
-    around = [(dx, dy) for dx in (-1, 0, 1) for dy in (-1, 0, 1) if dx or dy]
+    around = [(-1, 0), (1, 0), (0, -1), (0, 1)]
     barrier = pltpu.get_barrier_semaphore()
     for dx, dy in around:
         pl.semaphore_signal(barrier, inc=1, device_id=device(dx, dy), device_id_type=MESH)
@@ -186,13 +185,13 @@
         f = {q: start[q, here, :] for q in range(Q)}
         drag = 1.0 / (1.0 + resist[here, :])
         solid = mask[here, :].astype(F32)
-        rho, *u = moments(f, drag)
+        *u, rho = moments(f, drag)
         post = relax(f, rho, u, solid)
         for q in range(Q):
             p0[POST[q], there, :] = post[q]
         p0[DRAG, there, :] = drag
         p0[SOLID, there, :] = solid
-        for item, value in enumerate((rho, *u)):
+        for item, value in enumerate((*u, rho)):
             m0[item, there, :] = value
         return 0
 
@@ -233,49 +232,97 @@
         for place in range(PACK):
             packs[side, place] = sides[side][place]
 
+
     pl.semaphore_wait(barrier, len(around))
 
     copies = []
-
-    def send(src, dst, dx, dy):
+    first_x, last_x = gx == 0, gx == n_gx - 1
+    paired_up = lax.rem(gx, 2) == 0
+    paired_down = jnp.logical_not(paired_up)
+    along_x = jnp.logical_or(lax.rem(gx, 4) == 1, lax.rem(gx, 4) == 2)
+    along_z = jnp.logical_not(along_x)
+
+    def make(src, dst, dx, dy, sent_if=None, got_if=None):
         k = len(copies)
         copy = pltpu.make_async_remote_copy(
             src_ref=src, dst_ref=dst, send_sem=send_sem.at[k], recv_sem=recv_sem.at[k],
             device_id=device(dx, dy), device_id_type=MESH,
         )
-        copy.start()
-        copies.append(copy)
+        copies.append((copy, sent_if, got_if))
+        return copies[-1]
+
+    def only_if(condition, action):
+        if condition is None:
+            action()
+        else:
+            pl.when(condition)(action)
+
+    def start(*batch):
+        for copy, sent_if, _ in batch:
+            only_if(sent_if, copy.start)
+
+    def received(*batch):
+        for copy, _, got_if in batch:
+            only_if(got_if, copy.wait_recv)
+
+    def received_near(from_low, from_high):
+        pl.when(paired_up)(lambda: received(*from_high))
+        pl.when(paired_down)(lambda: received(*from_low))
+
+    def received_far(from_low, from_high):
+        pl.when(paired_up)(lambda: received(*from_low))
+        pl.when(paired_down)(lambda: received(*from_high))
+
+    def start_near(to_high, to_low):
+        pl.when(paired_up)(lambda: start(*to_high))
+        pl.when(paired_down)(lambda: start(*to_low))
+
+    def start_far(to_high, to_low):
+        pl.when(paired_up)(lambda: start(*to_low))
+        pl.when(paired_down)(lambda: start(*to_high))
 
     def span(ref, low, high, row, count):
         return ref.at[pl.ds(low, high - low), pl.ds((row + 8) * 8, count * 8), :]
 
-    def both(ref, low, high, row, count, dx):
-        send(span(ref, low, high, row, count), span(ref, low, high, row - 8 * dx, count), dx, 0)
-
-    for dx, dy in around:
-        if dy:
-            send(packs.at[(dy + 1) // 2], got.at[1 - dx, (1 - dy) // 2], dx, dy)
-    both(p0, 0, 21, 4, 4, 1)
-    both(p0, 0, 21, 0, 4, -1)
-    both(p0, 0, 16, 3, 1, 1)
-    both(p0, 5, 21, 4, 1, -1)
-    both(p0, 0, 5, 2, 1, 1)
-    both(p0, 16, 21, 5, 1, -1)
-    posts = len(copies)
-    both(q0, 0, 19, 6, 2, 1)
-    both(q0, 0, 19, 0, 2, -1)
-    both(q0, 5, 19, 5, 1, 1)
-    both(q0, 0, 14, 2, 1, -1)
-    both(q0, 14, 19, 4, 1, 1)
-    both(q0, 0, 5, 3, 1, -1)
+    def halo(ref, low, high, row, count, dx, *conditions):
+        there = span(ref, low, high, row - 8 * dx, count)
+        return make(span(ref, low, high, row, count), there, dx, 0, *conditions)
+
+    deep, shallow = (last_x, first_x), (jnp.logical_not(last_x), jnp.logical_not(first_x))
+
+    strips = [make(packs.at[(dy + 1) // 2], got.at[1, (1 - dy) // 2], 0, dy) for dy in (-1, 1)]
+    posts_low = (
+        halo(p0, 0, 19, 7, 1, 1), halo(p0, 19, 21, 5, 3, 1), halo(p0, 0, 14, 6, 1, 1), halo(p0, 0, 5, 5, 1, 1),
+    )
+    posts_high = (
+        halo(p0, 0, 19, 0, 1, -1), halo(p0, 19, 21, 0, 3, -1), halo(p0, 5, 19, 1, 1, -1), halo(p0, 14, 19, 2, 1, -1),
+    )
+    deeper = [
+        halo(p0, 14, 19, 6, 1, 1, *deep), halo(p0, 5, 19, 5, 1, 1, *deep), halo(p0, 19, 21, 3, 2, 1, *deep),
+        halo(p0, 0, 19, 4, 1, 1, *deep), halo(p0, 0, 14, 3, 1, 1, *deep), halo(p0, 0, 5, 2, 1, 1, *deep),
+    ]
+    adj_low = (halo(q0, 0, 19, 7, 1, 1), halo(q0, 0, 19, 6, 1, 1), halo(q0, 5, 19, 5, 1, 1), halo(q0, 14, 19, 4, 1, 1))
+    adj_high = (halo(q0, 0, 19, 0, 1, -1), halo(q0, 0, 19, 1, 1, -1), halo(q0, 0, 14, 2, 1, -1), halo(q0, 0, 5, 3, 1, -1))
+    mom_low = (halo(m3, 0, 3, 5, 3, 1, *shallow), halo(m2, 0, 3, 6, 1, 1, *shallow))
+    mom_high = (halo(m3, 0, 3, 0, 3, -1), halo(m2, 0, 3, 1, 1, -1))
+    relay_low = make(relay.at[1], got_relay.at[0], 1, 0, *shallow)
+    relay_high = make(relay.at[0], got_relay.at[1], -1, 0)
+    relay_deep = make(got.at[1], got.at[0], 1, 0, *deep)
+    edge_low = make(edges.at[1], got_edges.at[0], 1, 0, *shallow)
+    edge_high = make(edges.at[0], got_edges.at[1], -1, 0)
+
+    start(*strips)
+    start_far(posts_low, posts_high)
+    start_near(posts_low, posts_high)
+    start(*deeper)
 
     def forward(src, dst, mom, row):
         f = {
             q: shift_row(row_at(src, POST[q], row - LINKS[q][0]), LINKS[q][1], LINKS[q][2])
             for q in range(Q)
         }
-        rho, *u = moments(f, row_at(p0, DRAG, row))
-        for item, value in enumerate((rho, *u)):
+        *u, rho = moments(f, row_at(p0, DRAG, row))
+        for item, value in enumerate((*u, rho)):
             set_row(mom, item, row, value)
         if dst is not None:
             post = relax(f, rho, u, row_at(p0, SOLID, row))
@@ -287,7 +334,7 @@
             q: shift_row(row_at(src, ADJ[q], row + LINKS[q][0]), -LINKS[q][1], LINKS[q][2])
             for q in range(Q)
         }
-        rho, *u = [row_at(mom, item, row) for item in range(4)]
+        *u, rho = [row_at(mom, item, row) for item in range(4)]
         return pull(inc, rho, u, row_at(p0, DRAG, row), row_at(p0, SOLID, row))
 
     def middle(src, dst, mom, row):
@@ -297,53 +344,70 @@
         place = pl.ds(pl.multiple_of((row + 8) * 8, 8), 8)
         sums[place, :] = back if mom is m3 else sums[place, :] + back
 
-    def rows(body, low, high, *refs):
-        def one(row, _):
-            body(*refs, row)
+    def line(body, low, high, *refs):
+        def one(k, _):
+            body(*refs, jnp.where(paired_up, 7 - low - k, low + k))
             return 0
 
-        lax.fori_loop(low, high, one, 0, unroll=4)
-
-    def rim(body, low, high, *refs):
-        n = high - low
-
-        def one(k, _):
-            body(*refs, jnp.where(k < n, k + low, 7 - low + n - k))
-            return 0
-
-        lax.fori_loop(0, 2 * n, one, 0, unroll=4)
-
-    rows(forward, 1, 7, p0, p1, m1)
-    rows(forward, 2, 6, p1, p2, m2)
-    rows(forward, 3, 5, p2, None, m3)
-
-    for copy in copies[:posts]:
-        copy.wait_recv()
-    rim(forward, -5, 1, p0, p1, m1)
-    rim(forward, -4, 2, p1, p2, m2)
-    rim(forward, -3, 3, p2, None, m3)
-
+        lax.fori_loop(0, high - low, one, 0, unroll=min(4, high - low))
+
+    def final(row):
+        out, back = backward(q3, None, m0, row)
+        there = pl.ds(row, 8, stride=8)
+        for q in range(Q):
+            out_ref[q, there, :] = out[q]
+        grad_ref[there, :] = sums[pl.ds(pl.multiple_of((row + 8) * 8, 8), 8), :] + back
+
+    line(forward, 1, 7, p0, p1, m1)
+    line(forward, 2, 6, p1, p2, m2)
+    line(forward, 3, 5, p2, None, m3)
+
+    start_near(adj_low, adj_high)
+    pl.when(along_x)(lambda: start_far(adj_low[:1], adj_high[:1]))
+
+    received(*strips)
+    first_half = lax.broadcasted_iota(jnp.int32, (8, 128), 0) < 4
+    for place in range(PACK):
+        low, high = got[1, 0, place], got[1, 1, place]
+        relay[1, place] = jnp.where(first_half, pltpu.roll(low, 4, 0), high)
+        relay[0, place] = jnp.where(first_half, low, pltpu.roll(high, 4, 0))
+    start(relay_low, relay_high, relay_deep)
+    pl.when(along_x)(lambda: start_far(adj_low[1:], adj_high[1:]))
+
+    received_near(posts_low, posts_high)
+    line(forward, -2, 1, p0, p1, m1)
+    line(forward, -1, 2, p1, p2, m2)
+    line(forward, 0, 3, p2, None, m3)
+    start_near(mom_low, mom_high)
     left, right = mask_lanes(0, COLS, 64), mask_lanes(44, 44 + COLS, 64)
-
-    def halo_strip(strip, tile, item, slot, place):
-        by = slot * COLS
-        low = pltpu.roll(got[tile, 0, place], (-by) % 128, 1)
-        high = pltpu.roll(got[tile, 1, place], (44 - by) % 128, 1)
-        return jnp.where(left, low, jnp.where(right, high, strip))
-
-    def fill_strips(src, dst, first_item, count):
+    near, far = jnp.where(paired_up, 2, 0), jnp.where(paired_up, 0, 2)
+
+    def fill_strips(src, dst, first_item, count, tile):
         for item in range(count):
             slot, place = (first_item + item) % SLOTS, (first_item + item) // SLOTS
-            for tile in range(3):
-                strip = dst[item, 8:16, :] if tile == 1 else own_strip(src, item, tile)
-                dst[item, 8 * tile : 8 * tile + 8, :] = halo_strip(strip, tile, item, slot, place)
-
-    fill_strips(p0, s0, 0, ITEMS)
+            by = slot * COLS
+            here = pl.ds(pl.multiple_of(8 * tile, 8), 8)
+            strip = dst[item, 8:16, :] if isinstance(tile, int) else own_strip(src, item, tile)
+            low = pltpu.roll(got[tile, 0, place], (-by) % 128, 1)
+            high = pltpu.roll(got[tile, 1, place], (44 - by) % 128, 1)
+            dst[item, here, :] = jnp.where(left, low, jnp.where(right, high, strip))
+
+    def take_low():
+        received(relay_low)
+        for place in range(PACK):
+            both_sides = got_relay[0, place]
+            got[0, 0, place], got[0, 1, place] = pltpu.roll(both_sides, 4, 0), both_sides
+
+    def take_high():
+        received(relay_high)
+        for place in range(PACK):
+            both_sides = got_relay[1, place]
+            got[2, 0, place], got[2, 1, place] = both_sides, pltpu.roll(both_sides, 4, 0)
 
     def strip_forward(src, dst, mom):
         f = {q: shift_strip(src[POST[q]], *LINKS[q]) for q in range(Q)}
-        rho, *u = moments(f, s0[DRAG])
-        for item, value in enumerate((rho, *u)):
+        *u, rho = moments(f, s0[DRAG])
+        for item, value in enumerate((*u, rho)):
             mom[item] = value
         if dst is not None:
             post = relax(f, rho, u, s0[SOLID])
@@ -352,13 +416,28 @@
 
     for item in range(4):
         k0[item, 8:16, :] = own_strip(m0, item, 1)
-    strip_forward(s0, s1, k1)
-    strip_forward(s1, s2, k2)
-    strip_forward(s2, None, k3)
+
+    def strips_forward():
+        strip_forward(s0, s1, k1)
+        strip_forward(s1, s2, k2)
+        strip_forward(s2, None, k3)
+
+    def put_edges(side, wide, thin):
+        for item in range(3):
+            edges[side, 3 * item : 3 * item + 3, :] = k3[item, wide, :]
+            edges[side, 9 + item : 10 + item, :] = k2[item, thin, :]
+
+    def put_high():
+        put_edges(1, slice(13, 16), slice(14, 15))
+        start(edge_low)
+
+    def put_low():
+        put_edges(0, slice(8, 11), slice(9, 10))
+        start(edge_high)
 
     def strip_backward(src, mom):
         inc = {q: shift_strip(src[ADJ[q]], *[-c for c in LINKS[q]]) for q in range(Q)}
-        rho, *u = [mom[item] for item in range(4)]
+        *u, rho = [mom[item] for item in range(4)]
         return pull(inc, rho, u, s0[DRAG], s0[SOLID])
 
     def strip_middle(src, dst, mom):
@@ -367,42 +446,86 @@
             dst[ADJ[q]] = out[q]
         back_strip[...] = back if mom is k3 else back_strip[...] + back
 
-    rows(middle, 1, 7, q0, q1, m3)
-    rows(middle, 2, 6, q1, q2, m2)
-    rows(middle, 3, 5, q2, q3, m1)
-
-    for copy in copies[posts:]:
-        copy.wait_recv()
-    fill_strips(q0, t0, ITEMS, Q)
+    fill_strips(p0, s0, 0, ITEMS, 1)
+    fill_strips(q0, t0, ITEMS, Q, 1)
+
+    received_far(posts_low, posts_high)
+    pl.when(along_z)(lambda: start_far(adj_low, adj_high))
+    line(forward, 7, 10, p0, p1, m1)
+    line(forward, 6, 9, p1, p2, m2)
+    line(forward, 5, 8, p2, None, m3)
+    start_far(mom_low, mom_high)
+
+    pl.when(paired_up)(take_high)
+    pl.when(paired_down)(take_low)
+    fill_strips(p0, s0, 0, ITEMS, near)
+    pl.when(paired_down)(take_high)
+
+    @pl.when(jnp.logical_and(paired_up, shallow[1]))
+    def _():
+        take_low()
+
+    pl.when(shallow[1])(lambda: fill_strips(p0, s0, 0, ITEMS, far))
+    strips_forward()
+    put_high()
+    pl.when(shallow[1])(put_low)
+
+    received_near(adj_low, adj_high)
+    received_near(mom_low, mom_high)
+    line(middle, -3, 5, q0, q1, m3)
+    line(middle, -2, 4, q1, q2, m2)
+    line(middle, -1, 3, q2, q3, m1)
+    line(final, 0, 2)
+    fill_strips(q0, t0, ITEMS, Q, near)
+
+    line(middle, 5, 7, q0, q1, m3)
+    line(middle, 4, 6, q1, q2, m2)
+    line(middle, 3, 5, q2, q3, m1)
+    line(final, 2, 4)
+
+    received(*deeper, relay_deep)
+
+    @pl.when(first_x)
+    def _():
+        def at(lowest, *refs):
+            lax.fori_loop(0, 3, lambda k, _: (forward(*refs, k + lowest), 0)[1], 0, unroll=3)
+
+        at(-5, p0, p1, m1)
+        at(-4, p1, p2, m2)
+        at(-3, p2, None, m3)
+        fill_strips(p0, s0, 0, ITEMS, far)
+        strips_forward()
+        put_low()
+
+    received_far(adj_low, adj_high)
+    fill_strips(q0, t0, ITEMS, Q, far)
+
+    received_far(mom_low, mom_high)
+    received(edge_low, edge_high)
+
+    def take_edges(side, wide, thin):
+        for item in range(3):
+            k3[item, wide, :] = got_edges[side, 3 * item : 3 * item + 3, :]
+            k2[item, thin, :] = got_edges[side, 9 + item : 10 + item, :]
+
+    pl.when(shallow[1])(lambda: take_edges(0, slice(5, 8), slice(6, 7)))
+    take_edges(1, slice(16, 19), slice(17, 18))
+    line(middle, 7, 11, q0, q1, m3)
     strip_middle(t0, t1, k3)
+    line(middle, 6, 10, q1, q2, m2)
     strip_middle(t1, t2, k2)
+    line(middle, 5, 9, q2, q3, m1)
     strip_middle(t2, t3, k1)
     strip_out, strip_back = strip_backward(t3, k0)
     for q in range(Q):
         t1[ADJ[q], 8:16, :] = strip_out[q][8:16]
     back_strip[8:16, :] = back_strip[8:16, :] + strip_back[8:16]
-
-    rim(middle, -3, 1, q0, q1, m3)
-    rim(middle, -2, 2, q1, q2, m2)
-    rim(middle, -1, 3, q2, q3, m1)
-
-    def final(row, _):
-        out, back = backward(q3, None, m0, row)
-        there = pl.ds(row, 8, stride=8)
-        for q in range(Q):
-            out_ref[q, there, :] = out[q]
-        grad_ref[there, :] = row_at_sum(row) + back
-        return 0
-
-    def row_at_sum(row):
-        return sums[pl.ds(pl.multiple_of((row + 8) * 8, 8), 8), :]
-
-    lax.fori_loop(0, 8, final, 0, unroll=4)
-
-    edge_low, edge_high = mask_lanes(0, COLS, 128), mask_lanes(128 - COLS, 128, 128)
+    line(final, 4, 8)
+
+    first_cols, last_cols = mask_lanes(0, COLS, 128), mask_lanes(128 - COLS, 128, 128)
 
     def merge(ref, strip):
-        for k, lane, chosen in ((0, 6, edge_low), (4, 70, edge_low), (3, 38 - 122, edge_high), (7, 102 - 122, edge_high)):
+        for k, lane, chosen in ((0, 6, first_cols), (4, 70, first_cols), (3, 38 - 122, last_cols), (7, 102 - 122, last_cols)):
             here = slice(8 * k, 8 * k + 8)
             ref[here, :] = jnp.where(chosen, pltpu.roll(strip, (-lane) % 128, 1), ref[here, :])
 
@@ -410,8 +533,8 @@
         merge(out_ref.at[q], t1[ADJ[q], 8:16, :])
     merge(grad_ref, back_strip[8:16, :])
 
-    for copy in copies:
-        copy.wait_send()
+    for copy, sent_if, _ in copies:
+        only_if(sent_if, copy.wait_send)
 
 
 def to_tiles(a):
@@ -440,8 +563,8 @@
         out, grad = pl.pallas_call(
             functools.partial(kernel, n_gx, n_gy),
             out_shape=(
-                jax.ShapeDtypeStruct((Q, 64, 128), F32),
-                jax.ShapeDtypeStruct((64, 128), F32),
+                pltpu.VMEM((Q, 64, 128), F32),
+                pltpu.VMEM((64, 128), F32),
             ),
             in_specs=[any_space] * 4,
             out_specs=[vmem, vmem],
@@ -453,15 +576,16 @@
                 buf(ITEMS, 24, 128), buf(ITEMS, 24, 128), buf(ITEMS, 24, 128),
                 buf(Q, 24, 128), buf(Q, 24, 128), buf(Q, 24, 128), buf(Q, 24, 128),
                 buf(4, 24, 128), buf(4, 24, 128), buf(4, 24, 128), buf(4, 24, 128), buf(24, 128),
-                buf(2, PACK, 8, 128), buf(3, 2, PACK, 8, 128),
+                buf(2, PACK, 8, 128), buf(3, 2, PACK, 8, 128), buf(2, 16, 128), buf(2, 16, 128),
+                buf(2, PACK, 8, 128), buf(2, PACK, 8, 128),
                 pltpu.SemaphoreType.DMA((4,)),
-                pltpu.SemaphoreType.DMA((18,)),
-                pltpu.SemaphoreType.DMA((18,)),
+                pltpu.SemaphoreType.DMA((38,)),
+                pltpu.SemaphoreType.DMA((38,)),
             ],
             compiler_params=pltpu.CompilerParams(
-                collective_id=0, has_side_effects=True, vmem_limit_bytes=63 * 2**20
+                collective_id=0, has_side_effects=True, vmem_limit_bytes=48 * 2**20
             ),
-        )(to_tiles(start), to_tiles(final_adjoint), to_tiles(resist), to_tiles(mask))
+        )(*[pltpu.with_memory_space_constraint(to_tiles(a), pltpu.HBM) for a in (start, final_adjoint, resist, mask)])
         return from_tiles(out), from_tiles(grad)
 
     return jax.shard_map(

time: 32.9 us -> 27.3 us (0.83)
  Pallas kernels: 29.6 us -> 25.1 us
  local copies, waits for them, and re-layouts: 2.58 us -> 1.44 us
    pallas_call x1, Pallas kernels: 29.6 us -> 25.1 us  [local(): pl.pallas_call(functools.partial(kernel, n_gx, n_gy), out_shape=(pltpu.VM...]
    unnamed x4 -> x2, local copies, waits for them, and re-layouts: 2.58 us -> 1.44 us
where the time goes in v2:
time: 27.3 us; the launch traced here: 27.2 us
  Pallas kernels  25.1 us (92%)
  local copies, waits for them, and re-layouts  1.44 us (5%)
  between operations  0.64 us (2%)
    pallas_call x1, Pallas kernels, local(): pl.pallas_call(functools.partial(kernel, n_gx, n_gy), out_shape=(pltpu.VM...  25.1 us
    unnamed x2, local copies, waits for them, and re-layouts  1.44 us

profile of v2, /device:TPU:1, one launch (start us, length us, event | category | flops | bytes accessed | tf_op | source)
XLA Modules:
  0.0 27.2 jit_solution(12941586518969932862)
XLA Ops:
  0.6 25.1 %shard_map.59 = (f32[19,64,128]{2,1,0:T(8,128)S(1)}, f32[64,128]{1,0:T(8,128)S(1)}) custom-call(f32[19,64,128]{2,1,0:T(8,128)} %bitcast.32, f32[19,64,128]{2,1,0:T(8,128)} %bitcast.33, f32[64,128]{1,0:T(8,128)} %bitcast.34, s32[64,128]{1,0:T(8,128)} %bitcast.35), custom_call_target="tpu_custom_call" | custom-call | tf_op jit(solution)/shard_map/pallas_call | solution.py:563
  25.8 0.8 %copy.8 = f32[19,2,8,512]{3,2,1,0:T(8,128)} copy(f32[19,2,8,512]{3,2,1,0:T(8,128)S(1)} %bitcast.30) | data formatting | bytes 1245184
  26.6 0.6 %copy.9 = f32[2,8,512]{2,1,0:T(8,128)} copy(f32[2,8,512]{2,1,0:T(8,128)S(1)} %bitcast.31) | data formatting | bytes 65536

commit v3 on v2

--- a/solution.py
+++ b/solution.py
@@ -240,7 +240,7 @@
     paired_up = lax.rem(gx, 2) == 0
     paired_down = jnp.logical_not(paired_up)
     along_x = jnp.logical_or(lax.rem(gx, 4) == 1, lax.rem(gx, 4) == 2)
-    along_z = jnp.logical_not(along_x)
+    along_z = jnp.logical_and(jnp.logical_not(along_x), jnp.logical_not(last_x))
 
     def make(src, dst, dx, dy, sent_if=None, got_if=None):
         k = len(copies)
@@ -470,6 +470,7 @@
     put_high()
     pl.when(shallow[1])(put_low)
 
+    pl.when(last_x)(lambda: start_far(adj_low, adj_high))
     received_near(adj_low, adj_high)
     received_near(mom_low, mom_high)
     line(middle, -3, 5, q0, q1, m3)

time: 27.3 us -> 27.2 us (level)
  the two profiles are of different devices: /device:TPU:1 before, /device:TPU:0 now
where the time goes in v3:
time: 27.2 us; the launch traced here: 27.1 us
  Pallas kernels  25 us (92%)
  local copies, waits for them, and re-layouts  1.44 us (5%)
  between operations  0.64 us (2%)
    pallas_call x1, Pallas kernels, local(): pl.pallas_call(functools.partial(kernel, n_gx, n_gy), out_shape=(pltpu.VM...  25 us
    unnamed x2, local copies, waits for them, and re-layouts  1.44 us

profile of v3, /device:TPU:0, one launch (start us, length us, event | category | flops | bytes accessed | tf_op | source)
XLA Modules:
  0.0 27.1 jit_solution(13375323562814985934)
XLA Ops:
  0.6 25.0 %shard_map.59 = (f32[19,64,128]{2,1,0:T(8,128)S(1)}, f32[64,128]{1,0:T(8,128)S(1)}) custom-call(f32[19,64,128]{2,1,0:T(8,128)} %bitcast.32, f32[19,64,128]{2,1,0:T(8,128)} %bitcast.33, f32[64,128]{1,0:T(8,128)} %bitcast.34, s32[64,128]{1,0:T(8,128)} %bitcast.35), custom_call_target="tpu_custom_call" | custom-call | tf_op jit(solution)/shard_map/pallas_call | solution.py:564
  25.6 0.8 %copy.8 = f32[19,2,8,512]{3,2,1,0:T(8,128)} copy(f32[19,2,8,512]{3,2,1,0:T(8,128)S(1)} %bitcast.30) | data formatting | bytes 1245184
  26.5 0.6 %copy.9 = f32[2,8,512]{2,1,0:T(8,128)} copy(f32[2,8,512]{2,1,0:T(8,128)S(1)} %bitcast.31) | data formatting | bytes 65536
